TPU v7x, 32 devices: a whole 2x2x4 slice. The times are simulated.
32 devices in a mesh: phase: 2 (over x), blk: 4 (over z), tp: 4 (over y, core).
Axes of the slice: x: 2, y: 2, z: 4, core: 2. Of those that a mesh axis runs over, the one named last changes fastest.
Arguments:
- grid_lat: bfloat16 [8192, 512], P(('phase', 'blk')), may hold values from -6 to 6
- mesh_lat: bfloat16 [4096, 512], P('blk'), may hold values from -6 to 6
- mesh_cot: bfloat16 [4096, 512], P('blk'), may hold values from -6 to 6
- edge_lat: bfloat16 [4, 8192, 512], P(None, ('phase', 'blk')), may hold values from -6 to 6
- edge_slot: int32 [4, 8192], P(None, ('phase', 'blk')), may hold values from 0 to 127
- serve_list: int32 [2, 4, 4, 32], P('phase', 'blk'), may hold values from 0 to 1023
- w_grid: bfloat16 [512, 512], P('tp'), may hold values from -0.25 to 0.25
- w_mesh: bfloat16 [512, 512], P('tp'), may hold values from -0.25 to 0.25
- w_edge: bfloat16 [512, 512], P('tp'), may hold values from -0.25 to 0.25
- w_out: bfloat16 [512, 512], P('tp'), may hold values from -0.25 to 0.25
- bias: float32 [512], P('tp'), may hold values from -4 to 4
Outputs:
- grid_grad: bfloat16 [8192, 512], P(('phase', 'blk'), 'tp')
- mesh_grad: bfloat16 [4096, 512], P('blk', 'tp')
All inputs are finite; a program needn't handle non-finite values.
Results may differ from a plain program's by a relative error of at most 0.0051.
Values may be sent and summed in bfloat16 or wider, within the bound.
A program may use at most 64 MiB of HBM per device.

v0:
```python
import jax
import jax.numpy as jnp
from jax import lax
from jax.sharding import PartitionSpec as P


def silu_slope(value):
    sigma = jax.nn.sigmoid(value)
    return sigma * (1.0 + value * (1.0 - sigma))


def per_device(
    grid_lat,
    mesh_lat,
    mesh_cot,
    edge_lat,
    edge_slot,
    serve_list,
    w_grid,
    w_mesh,
    w_edge,
    w_out,
    bias,
):
    served = serve_list[0, 0]
    peers = served.shape[0]
    per_peer = served.shape[1]
    latent = mesh_lat.shape[1]
    sent_latent = mesh_lat[served]
    sent_grads = mesh_cot[served]
    got_latent, got_grads = (
        lax.all_to_all(sent_latent, "blk", split_axis=0, concat_axis=0, tiled=True),
        lax.all_to_all(sent_grads, "blk", split_axis=0, concat_axis=0, tiled=True),
    )
    slot_count = peers * per_peer
    got_latent = got_latent.reshape(slot_count, latent)
    got_grads = got_grads.reshape(slot_count, latent)
    mesh_pre = jnp.dot(got_latent, w_mesh.T, preferred_element_type=jnp.float32)
    act_grad = jnp.dot(got_grads, w_out.T, preferred_element_type=jnp.float32)
    grid_pre = jnp.dot(grid_lat, w_grid.T, preferred_element_type=jnp.float32)
    edge_pre = jnp.einsum("kgd,hd->kgh", edge_lat, w_edge, preferred_element_type=jnp.float32)
    preact = grid_pre[None] + mesh_pre[edge_slot] + edge_pre + bias
    pre_grad = act_grad[edge_slot] * silu_slope(preact)
    grid_sum = jnp.sum(pre_grad, axis=0).astype(jnp.bfloat16)
    slot_sum = jax.ops.segment_sum(
        pre_grad.reshape(-1, pre_grad.shape[2]), edge_slot.reshape(-1), num_segments=slot_count
    ).astype(jnp.bfloat16)
    grid_part = jnp.dot(grid_sum, w_grid, preferred_element_type=jnp.float32)
    slot_part = jnp.dot(slot_sum, w_mesh, preferred_element_type=jnp.float32)
    grid_share, slot_share = (
        lax.psum_scatter(grid_part, "tp", scatter_dimension=1, tiled=True),
        lax.psum_scatter(slot_part, "tp", scatter_dimension=1, tiled=True),
    )
    columns = slot_share.shape[1]
    returned = lax.all_to_all(
        slot_share.reshape(peers, per_peer, columns), "blk", split_axis=0, concat_axis=0, tiled=True
    )
    collected = jnp.zeros((mesh_lat.shape[0], columns), jnp.float32)
    collected = collected.at[served.reshape(-1)].add(returned.reshape(slot_count, columns))
    mesh_total = lax.psum(collected, "phase")
    return (grid_share.astype(jnp.bfloat16), mesh_total.astype(jnp.bfloat16))


def solution(mesh):
    in_specs = (
        P(("phase", "blk"), None),
        P("blk", None),
        P("blk", None),
        P(None, ("phase", "blk"), None),
        P(None, ("phase", "blk")),
        P("phase", "blk", None, None),
        P("tp", None),
        P("tp", None),
        P("tp", None),
        P("tp", None),
        P("tp"),
    )
    out_specs = (P(("phase", "blk"), "tp"), P("blk", "tp"))
    return jax.shard_map(
        per_device, mesh=mesh, in_specs=in_specs, out_specs=out_specs, check_vma=False
    )
```

profile of v0, /device:TPU:0, one launch (start us, length us, event | category | flops | bytes accessed | tf_op | source)
XLA Modules:
  0.0 146.5 jit_solution(14397396046629802816)
XLA Ops:
  7.2 0.0 copy-start
  7.2 0.0 copy-start.6
  7.2 0.0 copy-start.1
  7.2 0.0 copy-start.3
  7.2 0.8 compare_select_fusion.1
  8.0 0.1 reshape.84
  8.1 0.0 copy-start.5
  8.1 2.9 %gather_fusion = bf16[128,512]{1,0:T(8,128)(2,1)} fusion(bf16[1024,512]{1,0:T(8,128)(2,1)} %param.13, s32[1024]{0:T(1024)S(1)} %pad_clamp_fusion), kind=kCustom, calls=%fused_computation | custom fusion | bytes 262656 | tf_op jit(solution)/shard_map/gather | solution.py:30
  11.1 6.3 %all-to-all-start = ((bf16[4,32,512]{2,1,0:T(8,128)(2,1)}), bf16[4,32,512]{2,1,0:T(8,128)(2,1)S(1)}, u32[]{:S(2)}, u32[]{:S(2)}) async-start(bf16[4,32,512]{2,1,0:T(8,128)(2,1)} %bitcast.1), calls=%async_computation | async-start | bytes 262144 | tf_op jit(solution)/shard_map/all_to_all | solution.py:33
  17.4 0.7 fusion.9
  18.1 0.0 copy-done.1
  18.1 1.5 %gather_fusion.2 = bf16[128,512]{1,0:T(8,128)(2,1)} fusion(bf16[1024,512]{1,0:T(8,128)(2,1)S(1)} %copy-done.1, s32[1024]{0:T(1024)S(1)} %pad_clamp_fusion), kind=kCustom, calls=%fused_computation.2 | custom fusion | bytes 262656 | tf_op jit(solution)/shard_map/gather | solution.py:29
  19.6 0.0 copy-done.6
  19.6 0.0 copy-done
  19.6 0.0 copy-done.3
  19.6 1.2 fusion.13
  20.9 2.6 %all-to-all-done = bf16[4,32,512]{2,1,0:T(8,128)(2,1)S(1)} async-done(((bf16[4,32,512]{2,1,0:T(8,128)(2,1)}), bf16[4,32,512]{2,1,0:T(8,128)(2,1)S(1)}, u32[]{:S(2)}, u32[]{:S(2)}) %all-to-all-start) | async-done | bytes 131104 | tf_op jit(solution)/shard_map/all_to_all | solution.py:33
  23.5 3.3 %all-to-all-start.1 = ((bf16[4,32,512]{2,1,0:T(8,128)(2,1)}), bf16[4,32,512]{2,1,0:T(8,128)(2,1)S(1)}, u32[]{:S(2)}, u32[]{:S(2)}) async-start(bf16[4,32,512]{2,1,0:T(8,128)(2,1)} %bitcast.4), calls=%async_computation.1 | async-start | bytes 262144 | tf_op jit(solution)/shard_map/all_to_all | solution.py:32
  26.8 0.0 reduce-scatter.5.cloned.1.call-start
  26.8 0.0 copy-done.5
  26.9 0.2 fusion.12
  27.0 0.0 copy-start.2
  27.1 10.8 %gather_fusion.1 = f32[4096,128]{1,0:T(8,128)S(1)} fusion(f32[128,128]{1,0:T(8,128)S(1)} %fusion.12, s32[4096]{0:T(1024)S(1)} %bitcast_clamp_fusion), kind=kCustom, calls=%fused_computation.1 | custom fusion | bytes 4210688 | tf_op jit(solution)/shard_map/gather | solution.py:43
  37.8 0.0 all-to-all-done.1
  37.9 0.0 copy-done.2
  37.9 0.2 fusion.14
  38.1 0.0 copy-start.8
  38.1 14.2 %gather_fusion.3 = f32[4096,128]{1,0:T(8,128)} fusion(f32[128,128]{1,0:T(8,128)S(1)} %fusion.14, s32[4096]{0:T(1024)S(1)} %bitcast_clamp_fusion), kind=kCustom, calls=%fused_computation.3 | custom fusion | bytes 4210688 | tf_op jit(solution)/shard_map/gather | solution.py:42
  52.2 0.0 copy-done.8
  52.2 0.0 copy-start.4
  52.2 6.3 %fusion.11 = (bf16[1024,128]{1,0:T(8,128)(2,1)}, f32[4,1024,128]{2,1,0:T(8,128)}) fusion(f32[4,1024,128]{2,1,0:T(8,128)S(1)} %bitcast.38, f32[128]{0:T(128)S(1)} %copy-done.8, bf16[4,1024,512]{2,1,0:T(8,128)(2,1)} %param.14, bf16[128,512]{1,0:T(8,128)(2,1)} %param.19, f32[4,1024,128]{2,1,0:T(8,128)} %bitcast.39, f32[1024,128]{1,0:T(8,128)} %fusion.13), kind=kOutput, calls=%fused_computation.24 | convolution fusion | flops 543031296 | bytes 11403776 | tf_op jit(solution)/shard_map/kgd,hd->kgh/dot_general | solution.py:41
  58.6 22.7 %scatter_custom_fusion = f32[128,128]{1,0:T(8,128)S(1)} fusion(s32[4096]{0:T(1024)S(1)} %bitcast.45, f32[4096,128]{1,0:T(8,128)} %bitcast.46, f32[]{:T(128)} %constant.9.clone.1), kind=kCustom, calls=%fused_computation.15 | custom fusion | flops 524288 | bytes 66048 | tf_op jit(solution)/shard_map/scatter-add | solution.py:45
  81.3 0.9 fusion.5
  82.1 0.0 reduce-scatter.5.cloned.1.call-update
  82.2 0.0 reduce-scatter.3.cloned.1.call-start
  82.2 0.0 copy-done.4
  82.2 0.0 copy-start.7
  82.2 2.7 %fusion.15 = f32[1024,512]{1,0:T(8,128)} fusion(bf16[1024,128]{1,0:T(8,128)(2,1)} %get-tuple-element.2, bf16[128,512]{1,0:T(8,128)(2,1)S(1)} %copy-done.4), kind=kOutput, calls=%fused_computation.28 | convolution fusion | flops 134217728 | bytes 2490368 | tf_op jit(solution)/shard_map/dot_general | solution.py:48
  84.9 0.0 reduce-scatter.3.cloned.1.call-update
  85.0 0.0 copy-done.7
  85.0 0.1 reshape_squeeze.3
  85.1 18.7 %reduce-scatter.5.cloned.1.call-done = f32[128,128]{1,0:T(8,128)} async-done(((f32[128,512]{1,0:T(8,128)}), f32[128,128]{1,0:T(8,128)}) %reduce-scatter.5.cloned.1.call-update) | async-done | bytes 65552 | tf_op jit(solution)/shard_map/reduce_scatter | solution.py:52
  103.7 4.6 %all-to-all-start.2 = ((f32[4,32,128]{2,1,0:T(8,128)}), f32[4,32,128]{2,1,0:T(8,128)S(1)}, u32[]{:S(2)}, u32[]{:S(2)}) async-start(f32[4,32,128]{2,1,0:T(8,128)} %bitcast.42), calls=%async_computation.4 | async-start | bytes 131072 | tf_op jit(solution)/shard_map/all_to_all | solution.py:55
  108.3 5.7 %all-to-all-done.2 = f32[4,32,128]{2,1,0:T(8,128)S(1)} async-done(((f32[4,32,128]{2,1,0:T(8,128)}), f32[4,32,128]{2,1,0:T(8,128)S(1)}, u32[]{:S(2)}, u32[]{:S(2)}) %all-to-all-start.2) | async-done | bytes 65568 | tf_op jit(solution)/shard_map/all_to_all | solution.py:55
  114.1 1.1 scatter_custom_fusion.1
  115.2 16.1 %all-reduce.1 = bf16[1024,128]{1,0:T(8,128)(2,1)} all-reduce(f32[1024,128]{1,0:T(8,128)S(1)} %scatter_custom_fusion.1), channel_id=1, replica_groups=mesh['phase'=2,'blk'=4,'tp'=4] {'phase'}, use_global_device_ids=true, to_apply=%region_5.0 | all-reduce | flops 131072 | bytes 786432 | tf_op jit(solution)/shard_map/psum | solution.py:60
  131.3 6.6 %reduce-scatter.3.cloned.1.call-done = f32[1024,128]{1,0:T(8,128)} async-done(((f32[1024,512]{1,0:T(8,128)}), f32[1024,128]{1,0:T(8,128)}) %reduce-scatter.3.cloned.1.call-update) | async-done | bytes 524304 | tf_op jit(solution)/shard_map/reduce_scatter | solution.py:51
  137.9 1.8 %convert_element_type.13 = bf16[1024,128]{1,0:T(8,128)(2,1)} convert(f32[1024,128]{1,0:T(8,128)} %reduce-scatter.3.cloned.1.call-done) | non-fusion elementwise | flops 131072 | bytes 786432 | tf_op jit(solution)/shard_map/convert_element_type | solution.py:61
  (4 shorter events, 0.0 us)
Async XLA Ops:
  7.2 12.5 %copy-start = (bf16[1024,512]{1,0:T(8,128)(2,1)S(1)}, bf16[1024,512]{1,0:T(8,128)(2,1)}, u32[]{:S(2)}) copy-start(bf16[1024,512]{1,0:T(8,128)(2,1)} %param.11) | copy-start | bytes 3145732
  7.2 12.4 %copy-start.6 = (s32[4,1024]{1,0:T(4,128)S(1)}, s32[4,1024]{1,0:T(4,128)}, u32[]{:S(2)}) copy-start(s32[4,1024]{1,0:T(4,128)} %param.15) | copy-start | bytes 49156
  7.2 10.9 %copy-start.1 = (bf16[1024,512]{1,0:T(8,128)(2,1)S(1)}, bf16[1024,512]{1,0:T(8,128)(2,1)}, u32[]{:S(2)}) copy-start(bf16[1024,512]{1,0:T(8,128)(2,1)} %param.12) | copy-start | bytes 3145732
  7.2 12.4 %copy-start.3 = (bf16[128,512]{1,0:T(8,128)(2,1)S(1)}, bf16[128,512]{1,0:T(8,128)(2,1)}, u32[]{:S(2)}) copy-start(bf16[128,512]{1,0:T(8,128)(2,1)} %param.17) | copy-start | bytes 393220
  8.1 18.7 %copy-start.5 = (bf16[128,512]{1,0:T(8,128)(2,1)S(1)}, bf16[128,512]{1,0:T(8,128)(2,1)}, u32[]{:S(2)}) copy-start(bf16[128,512]{1,0:T(8,128)(2,1)} %param.20) | copy-start | bytes 393220
  11.1 12.4 %all-to-all-start = ((bf16[4,32,512]{2,1,0:T(8,128)(2,1)}), bf16[4,32,512]{2,1,0:T(8,128)(2,1)S(1)}, u32[]{:S(2)}, u32[]{:S(2)}) async-start(bf16[4,32,512]{2,1,0:T(8,128)(2,1)} %bitcast.1), calls=%async_computation | async-start | bytes 262144 | tf_op jit(solution)/shard_map/all_to_all | solution.py:33
  23.5 14.4 %all-to-all-start.1 = ((bf16[4,32,512]{2,1,0:T(8,128)(2,1)}), bf16[4,32,512]{2,1,0:T(8,128)(2,1)S(1)}, u32[]{:S(2)}, u32[]{:S(2)}) async-start(bf16[4,32,512]{2,1,0:T(8,128)(2,1)} %bitcast.4), calls=%async_computation.1 | async-start | bytes 262144 | tf_op jit(solution)/shard_map/all_to_all | solution.py:32
  26.8 76.9 %reduce-scatter.5.cloned.1.call-start = ((), (), s32[]{:S(2)}) async-start(), calls=%async_computation.6 | async-start | bytes 327680 | tf_op jit(solution)/shard_map/reduce_scatter | solution.py:52
  27.0 10.8 %copy-start.2 = (bf16[128,512]{1,0:T(8,128)(2,1)S(1)}, bf16[128,512]{1,0:T(8,128)(2,1)}, u32[]{:S(2)}) copy-start(bf16[128,512]{1,0:T(8,128)(2,1)} %param.18) | copy-start | bytes 393220
  38.1 14.2 %copy-start.8 = (f32[128]{0:T(128)S(1)}, f32[128]{0:T(128)}, u32[]{:S(2)}) copy-start(f32[128]{0:T(128)} %param.21) | copy-start | bytes 1540
  52.2 30.0 %copy-start.4 = (bf16[128,512]{1,0:T(8,128)(2,1)S(1)}, bf16[128,512]{1,0:T(8,128)(2,1)}, u32[]{:S(2)}) copy-start(bf16[128,512]{1,0:T(8,128)(2,1)} %param.17) | copy-start | bytes 393220
  82.2 55.7 %reduce-scatter.3.cloned.1.call-start = ((), (), s32[]{:S(2)}) async-start(), calls=%async_computation.5 | async-start | bytes 2621440 | tf_op jit(solution)/shard_map/reduce_scatter | solution.py:51
  82.2 2.7 %copy-start.7 = (s32[1,1,4,32]{3,2,1,0:T(4,128)S(1)}, s32[1,1,4,32]{3,2,1,0:T(4,128)}, u32[]{:S(2)}) copy-start(s32[1,1,4,32]{3,2,1,0:T(4,128)} %param.16) | copy-start | bytes 1540
  103.7 10.3 %all-to-all-start.2 = ((f32[4,32,128]{2,1,0:T(8,128)}), f32[4,32,128]{2,1,0:T(8,128)S(1)}, u32[]{:S(2)}, u32[]{:S(2)}) async-start(f32[4,32,128]{2,1,0:T(8,128)} %bitcast.42), calls=%async_computation.4 | async-start | bytes 131072 | tf_op jit(solution)/shard_map/all_to_all | solution.py:55
Sparse Core Ops, SparseCore 0:
  82.3 21.3 reduce-scatter.4
  106.4 31.4 reduce-scatter.2
where the time goes:
time: 147 us; the launch traced here: 146 us
  waiting for transfers between devices  33.6 us (23%)
  local copies, waits for them, and re-layouts  29.6 us (20%)
  other arithmetic  27.1 us (18%)
  blocking collectives  16.1 us (11%)
  starting transfers between devices  14.3 us (10%)
  between operations  14.2 us (10%)
  matrix products  11.5 us (8%)
    scatter-add x1, other arithmetic, per_device(): jax.ops.segment_sum(pre_grad.reshape(-1, pre_grad.shape[2]), edge_slot.re...  22.7 us
    reduce_scatter x1, waiting for transfers between devices, per_device(): lax.psum_scatter(slot_part, 'tp', scatter_dimension=1, tiled=True)  18.7 us
    psum x1, blocking collectives, per_device(): mesh_total = lax.psum(collected, 'phase')  16.1 us
    gather x1, local copies, waits for them, and re-layouts, per_device(): preact = grid_pre[None] + mesh_pre[edge_slot] + edge_pre + bias  14.2 us
    gather x1, local copies, waits for them, and re-layouts, per_device(): pre_grad = act_grad[edge_slot] * silu_slope(preact)  10.8 us
    reduce_scatter x1, waiting for transfers between devices, per_device(): lax.psum_scatter(grid_part, 'tp', scatter_dimension=1, tiled=True)  6.58 us
    dot_general x1, matrix products, per_device(): jnp.einsum('kgd,hd->kgh', edge_lat, w_edge, preferred_element_type=jnp.fl...  6.35 us
    all_to_all x1, starting transfers between devices, per_device(): lax.all_to_all(sent_grads, 'blk', split_axis=0, concat_axis=0, tiled=True)  6.32 us
  transfers between devices with their start and end apart: 5, of which 4 were waited for; matrix products, arithmetic and copies ran while one was open for 13% of the time, Pallas kernels for 0%

commit v1 on v0

v1 whole, which is shorter than its diff:
```python
import functools

import jax
import jax.numpy as jnp
from jax import lax
from jax.experimental import pallas as pl
from jax.experimental.pallas import tpu as pltpu
from jax.sharding import PartitionSpec as P

MESH_ID = pl.DeviceIdType.MESH
BF16 = jnp.bfloat16
F32 = jnp.float32
CHUNKS = 4
LANES = 128


def dot(a, b):
    return jnp.dot(a, b, preferred_element_type=F32)


def dot_nt(a, b):
    return lax.dot_general(a, b, (((1,), (1,)), ((), ())), preferred_element_type=F32)


def one_hot(cond):
    return jnp.where(cond, 1.0, 0.0).astype(BF16)


def as_column(row):
    return jnp.transpose(jnp.broadcast_to(row, (LANES, LANES)))


def slope_of(x):
    t = jnp.tanh(0.5 * x)
    sigma = 0.5 + 0.5 * t
    return sigma * (1.0 + x * (1.0 - sigma))


def kernel(
    dims,
    grid_hbm, mesh_hbm, cot_hbm, edge_hbm, slot_ref, serve_ref,
    wg_hbm, wm_hbm, we_hbm, wo_hbm, bias_ref,
    gout_hbm, mout_hbm,
    grid_v, mesh_v, cot_v, edge_v, wg_v, wm_v, we_v, wo_v,
    pick, tab_out, tab_in, serve_out, serve_in,
    wg_own, wg_sib, wm_out, wm_in,
    base_v, pre_v, hot, hot_t, gs_own, gs_sib, part_own, y_out, y_in,
    slot_out, slot_in, ret_out, ret_in, gout_v, mout_v,
    load_sem, edge_sem, store_sem,
    serve_s, serve_r, wg_s, wg_r, wm_s, wm_r, tab_s, tab_r,
    gs_s, gs_r, y_s, y_r, slot_s, slot_r, ret_s, ret_r,
):
    n_phase, n_blk, n_tp = dims
    n_y = n_tp // 2
    s, b, t = lax.axis_index("phase"), lax.axis_index("blk"), lax.axis_index("tp")
    y, core = lax.div(t, 2), lax.rem(t, 2)
    epg, rows, _ = edge_v.shape
    step = rows // CHUNKS
    nodes = mesh_v.shape[0]
    cap = serve_ref.shape[3]
    slots = n_blk * cap
    hid = wg_v.shape[0]
    feat = wg_own.shape[2]

    loads = []
    for i, (src, dst) in enumerate(
        [(mesh_hbm, mesh_v), (wm_hbm, wm_v), (cot_hbm, cot_v), (wo_hbm, wo_v),
         (wg_hbm, wg_v), (we_hbm, we_v), (grid_hbm, grid_v)]
    ):
        copy = pltpu.make_async_copy(src, dst, load_sem.at[i])
        copy.start()
        loads.append(copy)
    mesh_ld, wm_ld, cot_ld, wo_ld, wg_ld, we_ld, grid_ld = loads
    edge_ld = []
    for i in range(CHUNKS):
        part = pl.ds(i * step, step)
        copy = pltpu.make_async_copy(edge_hbm.at[:, part], edge_v.at[:, part], edge_sem.at[i])
        copy.start()
        edge_ld.append(copy)

    def remote(src, dst, send, recv, where):
        return pltpu.make_async_remote_copy(
            src_ref=src, dst_ref=dst, send_sem=send, recv_sem=recv,
            device_id=where, device_id_type=MESH_ID)

    barrier = pltpu.get_barrier_semaphore()
    others = [(i, j) for i in range(n_phase) for j in range(n_blk) if i or j]

    def shifted(i, j):
        return {"phase": lax.rem(s + i, n_phase), "blk": lax.rem(b + j, n_blk)}

    for d in range(1, n_tp):
        pl.semaphore_signal(barrier, inc=1, device_id={"tp": lax.rem(t + d, n_tp)}, device_id_type=MESH_ID)
    for i, j in others:
        pl.semaphore_signal(barrier, inc=1, device_id=shifted(i, j), device_id_type=MESH_ID)

    lane = lax.broadcasted_iota(jnp.int32, (LANES, LANES), 1)

    serve_row = jnp.concatenate([serve_ref[0, 0, i:i + 1, :] for i in range(n_blk)], axis=1)
    serve_out[...] = jnp.broadcast_to(serve_row, serve_out.shape)
    for i in range(slots // LANES):
        column = as_column(serve_row[:, i * LANES:(i + 1) * LANES])
        for j in range(nodes // LANES):
            pick[i * LANES:(i + 1) * LANES, j * LANES:(j + 1) * LANES] = one_hot(column == lane + j * LANES)
    mesh_ld.wait()
    lat = dot(pick[...], mesh_v[...]).astype(BF16)
    wm_ld.wait()
    mesh_pre = dot_nt(lat, wm_v[...]).astype(BF16)
    cot_ld.wait()
    cot = dot(pick[...], cot_v[...]).astype(BF16)
    wo_ld.wait()
    act = dot_nt(cot, wo_v[...]).astype(BF16)
    tab_out[:, :, :hid] = mesh_pre.reshape(n_blk, cap, hid)
    tab_out[:, :, hid:] = act.reshape(n_blk, cap, hid)
    tab_in[b] = tab_out[b]

    pl.semaphore_wait(barrier, n_tp - 1 + len(others))

    sends = []

    def send(copy):
        copy.start()
        sends.append(copy)
        return copy

    tab_cp = []
    for d in range(1, n_blk):
        to = lax.rem(b + d, n_blk)
        tab_cp.append(send(remote(tab_out.at[to], tab_in.at[b], tab_s.at[d], tab_r.at[d], {"blk": to})))

    wg_ld.wait()
    for j in range(n_tp):
        wg_own[j] = wg_v[:, j * feat:(j + 1) * feat]
        wm_out[j] = wm_v[:, j * feat:(j + 1) * feat]
    wm_in[t] = wm_out[t]
    sibling = {"tp": 2 * y + 1 - core}
    wg_cp = send(remote(wg_own, wg_sib, wg_s, wg_r, sibling))
    wm_cp = []
    for d in range(1, n_tp):
        to = lax.rem(t + d, n_tp)
        wm_cp.append(send(remote(wm_out.at[to], wm_in.at[t], wm_s.at[d], wm_r.at[d], {"tp": to})))
    serve_in[s] = serve_out[...]
    serve_cp = []
    for d in range(1, n_phase):
        to = lax.rem(s + d, n_phase)
        serve_cp.append(send(remote(serve_out, serve_in.at[s], serve_s.at[d], serve_r.at[d], {"phase": to})))

    def hot_body(i, carry):
        at = pl.ds(pl.multiple_of(i * LANES, LANES), LANES)
        for k in range(epg):
            row = slot_ref[k:k + 1, at]
            column = as_column(row)
            for j in range(slots // LANES):
                hot[k, at, j * LANES:(j + 1) * LANES] = one_hot(column == lane + j * LANES)
            hot_t[k, :, at] = one_hot(lax.broadcasted_iota(jnp.int32, (slots, LANES), 0) == row)
        return carry

    lax.fori_loop(0, rows // LANES, hot_body, 0)

    we_ld.wait()
    grid_ld.wait()
    for i in range(CHUNKS):
        edge_ld[i].wait()
        part = slice(i * step, (i + 1) * step)
        base_v[part, :] = dot_nt(grid_v[part, :], wg_v[...])
        for k in range(epg):
            pre_v[k, part, :] = dot_nt(edge_v[k, part, :], we_v[...])

    for cp in tab_cp:
        cp.wait_recv()
    table = tab_in[...].reshape(slots, 2 * hid)

    gs_cp, y_cp = [], []

    def cross(i):
        gs_cp[i].wait_recv()
        mine, theirs = gs_own[i], gs_sib[i]
        for d in range(n_y):
            to = 2 * lax.rem(y + d, n_y) + core
            share = dot(mine, wg_own[to]) + dot(theirs, wg_sib[to])
            if d == 0:
                part_own[i] = share
            else:
                y_out[d - 1, i] = share.astype(BF16)
                y_cp.append((d, i, send(remote(
                    y_out.at[d - 1, i], y_in.at[d - 1, i], y_s.at[d - 1, i], y_r.at[d - 1, i], {"tp": to}))))

    slot_total = jnp.zeros((slots, hid), F32)
    for i in range(CHUNKS):
        part = slice(i * step, (i + 1) * step)
        total = jnp.zeros((step, hid), F32)
        base = base_v[part, :] + bias_ref[...]
        for k in range(epg):
            got = dot(hot[k, part, :], table)
            slope = slope_of(pre_v[k, part, :] + base + got[:, :hid])
            total = total + got[:, hid:] * slope
            slot_total = slot_total + dot(hot_t[k, :, part], slope.astype(BF16))
        gs_own[i] = total.astype(BF16)
        gs_cp.append(send(remote(gs_own.at[i], gs_sib.at[i], gs_s.at[i], gs_r.at[i], sibling)))
        if i == 0:
            wg_cp.wait_recv()
        else:
            cross(i - 1)

    slot_out[...] = (slot_total * table[:, hid:].astype(F32)).astype(BF16)
    slot_in[t] = slot_out[...]
    slot_cp = []
    for d in range(1, n_tp):
        slot_cp.append(send(remote(
            slot_out, slot_in.at[t], slot_s.at[d], slot_r.at[d], {"tp": lax.rem(t + d, n_tp)})))
    cross(CHUNKS - 1)

    for cp in wm_cp:
        cp.wait_recv()
    for cp in slot_cp:
        cp.wait_recv()
    share = dot(slot_in[0], wm_in[0])
    for j in range(1, n_tp):
        share = share + dot(slot_in[j], wm_in[j])
    ret_out[...] = share.astype(BF16).reshape(n_blk, cap, feat)
    ret_in[s, b] = ret_out[b]
    ret_cp = []
    for n, (i, j) in enumerate(others):
        where = shifted(i, j)
        ret_cp.append(send(remote(
            ret_out.at[where["blk"]], ret_in.at[s, b], ret_s.at[n], ret_r.at[n], where)))

    stores = []
    for i in range(CHUNKS):
        value = part_own[i]
        for d, at, cp in y_cp:
            if at == i:
                cp.wait_recv()
                value = value + y_in[d - 1, i].astype(F32)
        part = pl.ds(i * step, step)
        gout_v[i * step:(i + 1) * step, :] = value.astype(BF16)
        copy = pltpu.make_async_copy(gout_v.at[part], gout_hbm.at[part], store_sem.at[i])
        copy.start()
        stores.append(copy)

    for cp in serve_cp:
        cp.wait_recv()
    for cp in ret_cp:
        cp.wait_recv()
    node = lax.broadcasted_iota(jnp.int32, (nodes, slots), 0)
    value = None
    for i in range(n_phase):
        spread = one_hot(node == serve_in[i, 0:1, :])
        more = dot(spread, ret_in[i].reshape(slots, feat))
        value = more if value is None else value + more
    mout_v[...] = value.astype(BF16)
    copy = pltpu.make_async_copy(mout_v, mout_hbm, store_sem.at[CHUNKS])
    copy.start()
    stores.append(copy)

    for cp in sends:
        cp.wait_send()
    for copy in stores:
        copy.wait()


def per_device(dims, grid_lat, mesh_lat, mesh_cot, edge_lat, edge_slot, serve_list, w_grid, w_mesh, w_edge, w_out, bias):
    n_phase, n_blk, n_tp = dims
    n_y = n_tp // 2
    epg, rows, lat = edge_lat.shape
    nodes = mesh_lat.shape[0]
    cap = serve_list.shape[3]
    slots = n_blk * cap
    hid = w_grid.shape[0]
    feat = lat // n_tp
    step = rows // CHUNKS
    n_other = n_phase * n_blk - 1
    vmem = pltpu.VMEM
    dma = pltpu.SemaphoreType.DMA
    hbm_spec = pl.BlockSpec(memory_space=pl.ANY)
    vmem_spec = pl.BlockSpec(memory_space=pltpu.VMEM)
    return pl.pallas_call(
        functools.partial(kernel, dims),
        out_shape=(
            jax.ShapeDtypeStruct((rows, feat), BF16),
            jax.ShapeDtypeStruct((nodes, feat), BF16),
        ),
        in_specs=[hbm_spec] * 4 + [vmem_spec] * 2 + [hbm_spec] * 4 + [vmem_spec],
        out_specs=(hbm_spec, hbm_spec),
        scratch_shapes=[
            vmem((rows, lat), BF16), vmem((nodes, lat), BF16), vmem((nodes, lat), BF16),
            vmem((epg, rows, lat), BF16),
            vmem((hid, lat), BF16), vmem((hid, lat), BF16), vmem((hid, lat), BF16), vmem((hid, lat), BF16),
            vmem((slots, nodes), BF16),
            vmem((n_blk, cap, 2 * hid), BF16), vmem((n_blk, cap, 2 * hid), BF16),
            vmem((8, slots), jnp.int32), vmem((n_phase, 8, slots), jnp.int32),
            vmem((n_tp, hid, feat), BF16), vmem((n_tp, hid, feat), BF16),
            vmem((n_tp, hid, feat), BF16), vmem((n_tp, hid, feat), BF16),
            vmem((rows, hid), F32), vmem((epg, rows, hid), F32),
            vmem((epg, rows, slots), BF16), vmem((epg, slots, rows), BF16),
            vmem((CHUNKS, step, hid), BF16), vmem((CHUNKS, step, hid), BF16),
            vmem((CHUNKS, step, feat), F32),
            vmem((max(n_y - 1, 1), CHUNKS, step, feat), BF16), vmem((max(n_y - 1, 1), CHUNKS, step, feat), BF16),
            vmem((slots, hid), BF16), vmem((n_tp, slots, hid), BF16),
            vmem((n_blk, cap, feat), BF16), vmem((n_phase, n_blk, cap, feat), BF16),
            vmem((rows, feat), BF16), vmem((nodes, feat), BF16),
            dma((7,)), dma((CHUNKS,)), dma((CHUNKS + 1,)),
            dma((n_phase,)), dma((n_phase,)), dma, dma, dma((n_tp,)), dma((n_tp,)), dma((n_blk,)), dma((n_blk,)),
            dma((CHUNKS,)), dma((CHUNKS,)), dma((max(n_y - 1, 1), CHUNKS)), dma((max(n_y - 1, 1), CHUNKS)),
            dma((n_tp,)), dma((n_tp,)), dma((n_other,)), dma((n_other,)),
        ],
        compiler_params=pltpu.CompilerParams(
            collective_id=0, has_side_effects=True, vmem_limit_bytes=56 * 1024 * 1024),
    )(grid_lat, mesh_lat, mesh_cot, edge_lat, edge_slot, serve_list,
      w_grid, w_mesh, w_edge, w_out, bias.reshape(1, hid))


def solution(mesh):
    dims = (mesh.shape["phase"], mesh.shape["blk"], mesh.shape["tp"])
    in_specs = (
        P(("phase", "blk"), None),
        P("blk", None),
        P("blk", None),
        P(None, ("phase", "blk"), None),
        P(None, ("phase", "blk")),
        P("phase", "blk", None, None),
        P("tp", None),
        P("tp", None),
        P("tp", None),
        P("tp", None),
        P("tp"),
    )
    out_specs = (P(("phase", "blk"), "tp"), P("blk", "tp"))
    return jax.shard_map(
        functools.partial(per_device, dims), mesh=mesh, in_specs=in_specs, out_specs=out_specs, check_vma=False
    )
```

time: 147 us -> 30.8 us (0.21)
  waiting for transfers between devices: 33.6 us -> 0 us
  other arithmetic: 27.1 us -> 0 us
  Pallas kernels: 0 us -> 26.6 us
  local copies, waits for them, and re-layouts: 29.6 us -> 3.34 us
  blocking collectives: 16.1 us -> 0 us
  starting transfers between devices: 14.3 us -> 0 us
  between operations: 14.2 us -> 0.64 us
  matrix products: 11.5 us -> 0 us
    gather x4 -> x0, local copies, waits for them, and re-layouts: 29.4 us -> none  [the longest x1 14.2 us: per_device(): preact = grid_pre[None] + mesh_pre[edge_slot] + edge_pre + bias]
    pallas_call x0 -> x1, Pallas kernels: none -> 26.6 us  [per_device(): pl.pallas_call(functools.partial(kernel, dims), out_shape=(jax.ShapeDtype...]
    reduce_scatter x2 -> x0, waiting for transfers between devices: 25.3 us -> none  [the longest x1 18.7 us: per_device(): lax.psum_scatter(slot_part, 'tp', scatter_dimension=1, tiled=True)]
    scatter-add x2 -> x0, other arithmetic: 23.8 us -> none  [the longest x1 22.7 us: per_device(): jax.ops.segment_sum(pre_grad.reshape(-1, pre_grad.shape[2]), edge_slot.re...]
    psum x1 -> x0, blocking collectives: 16.1 us -> none  [per_device(): mesh_total = lax.psum(collected, 'phase')]
    all_to_all x3 -> x0, starting transfers between devices: 14.2 us -> none  [the longest x1 6.32 us: per_device(): lax.all_to_all(sent_grads, 'blk', split_axis=0, concat_axis=0, tiled=True)]
    dot_general x6 -> x0, matrix products: 11.5 us -> none  [the longest x1 6.35 us: per_device(): jnp.einsum('kgd,hd->kgh', edge_lat, w_edge, preferred_element_type=jnp.fl...]
    all_to_all x3 -> x0, waiting for transfers between devices: 8.32 us -> none  [the longest x1 5.74 us: per_device(): lax.all_to_all(slot_share.reshape(peers, per_peer, columns), 'blk', split...]
  transfers between devices with their start and end apart: 5 -> 0, of which waited for: 4 -> 0; matrix products, arithmetic and copies ran while one was open for 13% -> 0% of each run, Pallas kernels for 0% -> 0%
where the time goes in v1:
time: 30.8 us; the launch traced here: 30.6 us
  Pallas kernels  26.6 us (86%)
  local copies, waits for them, and re-layouts  3.34 us (11%)
  between operations  0.64 us (2%)
    pallas_call x1, Pallas kernels, per_device(): pl.pallas_call(functools.partial(kernel, dims), out_shape=(jax.ShapeDtype...  26.6 us
    unnamed x2, local copies, waits for them, and re-layouts  3.34 us

profile of v1, /device:TPU:0, one launch (start us, length us, event | category | flops | bytes accessed | tf_op | source)
XLA Modules:
  0.0 30.6 jit_solution(10463133423777470621)
XLA Ops:
  0.6 26.6 %shard_map.122 = (bf16[1024,128]{1,0:T(8,128)(2,1)}, bf16[1024,128]{1,0:T(8,128)(2,1)}) custom-call(bf16[1024,512]{1,0:T(8,128)(2,1)} %grid_hbm.1, bf16[1024,512]{1,0:T(8,128)(2,1)} %mesh_hbm.1, bf16[1024,512]{1,0:T(8,128)(2,1)} %cot_hbm.1, bf16[4,1024,512]{2,1,0:T(8,128)(2,1)} %edge_hbm.1, s32[4,1024]{1,0:T(4,128)} %slot_ref.1, s32[1,1,4,32]{3,2,1,0:T(4,128)} %serve_ref.1, ...), custom_call_target="tpu_custom_call" | custom-call | tf_op jit(solution)/shard_map/pallas_call | solution.py:277
  27.2 1.7 %copy.15 = bf16[1024,128]{1,0:T(8,128)(2,1)} copy(bf16[1024,128]{1,0:T(8,128)(2,1)} %get-tuple-element.4) | data formatting | bytes 524288
  28.9 1.7 %copy.16 = bf16[1024,128]{1,0:T(8,128)(2,1)} copy(bf16[1024,128]{1,0:T(8,128)(2,1)} %get-tuple-element.5) | data formatting | bytes 524288

commit v2 on v1

--- a/solution.py
+++ b/solution.py
@@ -197,10 +197,6 @@
             slot_total = slot_total + dot(hot_t[k, :, part], slope.astype(BF16))
         gs_own[i] = total.astype(BF16)
         gs_cp.append(send(remote(gs_own.at[i], gs_sib.at[i], gs_s.at[i], gs_r.at[i], sibling)))
-        if i == 0:
-            wg_cp.wait_recv()
-        else:
-            cross(i - 1)
 
     slot_out[...] = (slot_total * table[:, hid:].astype(F32)).astype(BF16)
     slot_in[t] = slot_out[...]
@@ -208,7 +204,9 @@
     for d in range(1, n_tp):
         slot_cp.append(send(remote(
             slot_out, slot_in.at[t], slot_s.at[d], slot_r.at[d], {"tp": lax.rem(t + d, n_tp)})))
-    cross(CHUNKS - 1)
+    wg_cp.wait_recv()
+    for i in range(CHUNKS):
+        cross(i)
 
     for cp in wm_cp:
         cp.wait_recv()
@@ -257,6 +255,11 @@
         cp.wait_send()
     for copy in stores:
         copy.wait()
+
+
+def tail_kernel(grid_ref, mesh_ref, grid_out, mesh_out):
+    grid_out[...] = grid_ref[...]
+    mesh_out[...] = mesh_ref[...]
 
 
 def per_device(dims, grid_lat, mesh_lat, mesh_cot, edge_lat, edge_slot, serve_list, w_grid, w_mesh, w_edge, w_out, bias):
@@ -274,7 +277,7 @@
     dma = pltpu.SemaphoreType.DMA
     hbm_spec = pl.BlockSpec(memory_space=pl.ANY)
     vmem_spec = pl.BlockSpec(memory_space=pltpu.VMEM)
-    return pl.pallas_call(
+    grid_out, mesh_out = pl.pallas_call(
         functools.partial(kernel, dims),
         out_shape=(
             jax.ShapeDtypeStruct((rows, feat), BF16),
@@ -308,6 +311,15 @@
             collective_id=0, has_side_effects=True, vmem_limit_bytes=56 * 1024 * 1024),
     )(grid_lat, mesh_lat, mesh_cot, edge_lat, edge_slot, serve_list,
       w_grid, w_mesh, w_edge, w_out, bias.reshape(1, hid))
+    return pl.pallas_call(
+        tail_kernel,
+        out_shape=(
+            jax.ShapeDtypeStruct((rows, feat), BF16),
+            jax.ShapeDtypeStruct((nodes, feat), BF16),
+        ),
+        in_specs=[vmem_spec] * 2,
+        out_specs=(vmem_spec, vmem_spec),
+    )(grid_out, mesh_out)
 
 
 def solution(mesh):

time: 30.8 us -> 27.1 us (0.88)
  local copies, waits for them, and re-layouts: 3.34 us -> 0 us
  Pallas kernels: 26.6 us -> 26.2 us
    unnamed x2 -> x0, local copies, waits for them, and re-layouts: 3.34 us -> none
    pallas_call x1, Pallas kernels: 26.6 us -> 24.4 us  [per_device(): pl.pallas_call(functools.partial(kernel, dims), out_shape=(jax.ShapeDtype...]
    pallas_call x0 -> x1, Pallas kernels: none -> 1.84 us  [per_device(): pl.pallas_call(tail_kernel, out_shape=(jax.ShapeDtypeStruct((rows, feat),...]
where the time goes in v2:
time: 27.1 us; the launch traced here: 26.9 us
  Pallas kernels  26.2 us (97%)
  between operations  0.64 us (2%)
    pallas_call x1, Pallas kernels, per_device(): pl.pallas_call(functools.partial(kernel, dims), out_shape=(jax.ShapeDtype...  24.4 us
    pallas_call x1, Pallas kernels, per_device(): pl.pallas_call(tail_kernel, out_shape=(jax.ShapeDtypeStruct((rows, feat),...  1.84 us

profile of v2, /device:TPU:0, one launch (start us, length us, event | category | flops | bytes accessed | tf_op | source)
XLA Modules:
  0.0 26.9 jit_solution(6806326893068952878)
XLA Ops:
  0.6 24.4 %shard_map.122 = (bf16[1024,128]{1,0:T(8,128)(2,1)}, bf16[1024,128]{1,0:T(8,128)(2,1)}) custom-call(bf16[1024,512]{1,0:T(8,128)(2,1)} %grid_hbm.1, bf16[1024,512]{1,0:T(8,128)(2,1)} %mesh_hbm.1, bf16[1024,512]{1,0:T(8,128)(2,1)} %cot_hbm.1, bf16[4,1024,512]{2,1,0:T(8,128)(2,1)} %edge_hbm.1, s32[4,1024]{1,0:T(4,128)} %slot_ref.1, s32[1,1,4,32]{3,2,1,0:T(4,128)} %serve_ref.1, ...), custom_call_target="tpu_custom_call" | custom-call | tf_op jit(solution)/shard_map/pallas_call | solution.py:280
  25.0 1.8 %shard_map.123 = (bf16[1024,128]{1,0:T(8,128)(2,1)}, bf16[1024,128]{1,0:T(8,128)(2,1)}) custom-call(bf16[1024,128]{1,0:T(8,128)(2,1)} %get-tuple-element.4.grid_ref, bf16[1024,128]{1,0:T(8,128)(2,1)} %get-tuple-element.5.mesh_ref), custom_call_target="tpu_custom_call" | custom-call | tf_op jit(solution)/shard_map/pallas_call | solution.py:314

commit v3 on v2

--- a/solution.py
+++ b/solution.py
@@ -44,7 +44,7 @@
     grid_v, mesh_v, cot_v, edge_v, wg_v, wm_v, we_v, wo_v,
     pick, tab_out, tab_in, serve_out, serve_in,
     wg_own, wg_sib, wm_out, wm_in,
-    base_v, pre_v, hot, hot_t, gs_own, gs_sib, part_own, y_out, y_in,
+    base_v, pre_v, hot, hot_t, got_v, slope_v, gs_own, gs_sib, part_own, y_out, y_in,
     slot_out, slot_in, ret_out, ret_in, gout_v, mout_v,
     load_sem, edge_sem, store_sem,
     serve_s, serve_r, wg_s, wg_r, wm_s, wm_r, tab_s, tab_r,
@@ -152,7 +152,7 @@
             column = as_column(row)
             for j in range(slots // LANES):
                 hot[k, at, j * LANES:(j + 1) * LANES] = one_hot(column == lane + j * LANES)
-            hot_t[k, :, at] = one_hot(lax.broadcasted_iota(jnp.int32, (slots, LANES), 0) == row)
+            hot_t[:, pl.ds(pl.multiple_of(k * rows + i * LANES, LANES), LANES)] = one_hot(lax.broadcasted_iota(jnp.int32, (slots, LANES), 0) == row)
         return carry
 
     lax.fori_loop(0, rows // LANES, hot_body, 0)
@@ -185,19 +185,20 @@
                 y_cp.append((d, i, send(remote(
                     y_out.at[d - 1, i], y_in.at[d - 1, i], y_s.at[d - 1, i], y_r.at[d - 1, i], {"tp": to}))))
 
-    slot_total = jnp.zeros((slots, hid), F32)
+    for k in range(epg):
+        got_v[k] = dot(hot[k], table)
     for i in range(CHUNKS):
         part = slice(i * step, (i + 1) * step)
         total = jnp.zeros((step, hid), F32)
         base = base_v[part, :] + bias_ref[...]
         for k in range(epg):
-            got = dot(hot[k, part, :], table)
-            slope = slope_of(pre_v[k, part, :] + base + got[:, :hid])
-            total = total + got[:, hid:] * slope
-            slot_total = slot_total + dot(hot_t[k, :, part], slope.astype(BF16))
+            slope = slope_of(pre_v[k, part, :] + base + got_v[k, part, :hid])
+            total = total + got_v[k, part, hid:] * slope
+            slope_v[k * rows + i * step:k * rows + (i + 1) * step, :] = slope.astype(BF16)
         gs_own[i] = total.astype(BF16)
         gs_cp.append(send(remote(gs_own.at[i], gs_sib.at[i], gs_s.at[i], gs_r.at[i], sibling)))
 
+    slot_total = dot(hot_t[...], slope_v[...])
     slot_out[...] = (slot_total * table[:, hid:].astype(F32)).astype(BF16)
     slot_in[t] = slot_out[...]
     slot_cp = []
@@ -295,7 +296,7 @@
             vmem((n_tp, hid, feat), BF16), vmem((n_tp, hid, feat), BF16),
             vmem((n_tp, hid, feat), BF16), vmem((n_tp, hid, feat), BF16),
             vmem((rows, hid), F32), vmem((epg, rows, hid), F32),
-            vmem((epg, rows, slots), BF16), vmem((epg, slots, rows), BF16),
+            vmem((epg, rows, slots), BF16), vmem((slots, epg * rows), BF16), vmem((epg, rows, 2 * hid), F32), vmem((epg * rows, hid), BF16),
             vmem((CHUNKS, step, hid), BF16), vmem((CHUNKS, step, hid), BF16),
             vmem((CHUNKS, step, feat), F32),
             vmem((max(n_y - 1, 1), CHUNKS, step, feat), BF16), vmem((max(n_y - 1, 1), CHUNKS, step, feat), BF16),

time: 27.1 us -> 25.4 us (0.937)
  Pallas kernels: 26.2 us -> 24.6 us
    pallas_call x1, Pallas kernels: 24.4 us -> 22.8 us  [per_device(): pl.pallas_call(functools.partial(kernel, dims), out_shape=(jax.ShapeDtype...]
where the time goes in v3:
time: 25.4 us; the launch traced here: 25.2 us
  Pallas kernels  24.6 us (97%)
  between operations  0.64 us (3%)
    pallas_call x1, Pallas kernels, per_device(): pl.pallas_call(functools.partial(kernel, dims), out_shape=(jax.ShapeDtype...  22.8 us
    pallas_call x1, Pallas kernels, per_device(): pl.pallas_call(tail_kernel, out_shape=(jax.ShapeDtypeStruct((rows, feat),...  1.84 us

profile of v3, /device:TPU:0, one launch (start us, length us, event | category | flops | bytes accessed | tf_op | source)
XLA Modules:
  0.0 25.2 jit_solution(3241982969196365545)
XLA Ops:
  0.6 22.8 %shard_map.122 = (bf16[1024,128]{1,0:T(8,128)(2,1)}, bf16[1024,128]{1,0:T(8,128)(2,1)}) custom-call(bf16[1024,512]{1,0:T(8,128)(2,1)} %grid_hbm.1, bf16[1024,512]{1,0:T(8,128)(2,1)} %mesh_hbm.1, bf16[1024,512]{1,0:T(8,128)(2,1)} %cot_hbm.1, bf16[4,1024,512]{2,1,0:T(8,128)(2,1)} %edge_hbm.1, s32[4,1024]{1,0:T(4,128)} %slot_ref.1, s32[1,1,4,32]{3,2,1,0:T(4,128)} %serve_ref.1, ...), custom_call_target="tpu_custom_call" | custom-call | tf_op jit(solution)/shard_map/pallas_call | solution.py:281
  23.4 1.8 %shard_map.123 = (bf16[1024,128]{1,0:T(8,128)(2,1)}, bf16[1024,128]{1,0:T(8,128)(2,1)}) custom-call(bf16[1024,128]{1,0:T(8,128)(2,1)} %get-tuple-element.4.grid_ref, bf16[1024,128]{1,0:T(8,128)(2,1)} %get-tuple-element.5.mesh_ref), custom_call_target="tpu_custom_call" | custom-call | tf_op jit(solution)/shard_map/pallas_call | solution.py:315
